TPU v7x, 128 devices: a whole 4x4x4 slice. The times are simulated.
128 devices in a mesh: inst: 8 (over x, y_lo), span: 16 (over z, y_hi, core).
Axes of the slice: x: 4, y: 4 (y_hi: 2, y_lo: 2; y = y_hi * 2 + y_lo), z: 4, core: 2. Of those that a mesh axis runs over, the one named last changes fastest.
Arguments:
- adjoint_start: float32 [32, 4, 49152], P('inst', None, 'span'), may hold values from -6 to 6
- source: float32 [32, 4, 49152], P('inst', None, 'span'), may hold values from -6 to 6
- jacobian_tiles: bfloat16 [32, 192, 3, 256, 256], P('inst', 'span'), may hold values from -0.21875 to 0.21875
- tile_columns: int32 [192, 3], P('span'), may hold values from -1 to 12
- pseudo_time: float32 [49152], P('span'), may hold values from 0.5 to 4
- control_terms: float32 [3, 32, 49152], P(None, 'inst', 'span'), may hold values from -4 to 4
- surface_rows: int32 [12288], P('span'), may hold values from 0 to 3071
- surface_weight: float32 [3, 12288], replicated, may hold values from -0.009765625 to 0.009765625
- trim_inverse: float32 [3, 3], replicated, may hold values from -4 to 4
Outputs:
- adjoint: float32 [32, 4, 49152], P('inst', None, 'span')
- residual: float32 [32, 4, 49152], P('inst', None, 'span')
Inputs may be any that keep to these rules, and one draw needn't show every extreme that they name: `tile_columns`: -1 names the last block row of the span block before, 12 the first of the next. `surface_rows`: a row of the entry's own span block.
All inputs are finite; a program needn't handle non-finite values.
Results may differ from a plain program's by a relative error of at most 0.0016.
Values may be sent and summed in bfloat16 or wider, within the bound.
A program may use at most 128 MiB of HBM per device.

v0:
```python
import math

import jax
import jax.numpy as jnp
from jax import lax
from jax.sharding import PartitionSpec as P

INSTANCES = 32
SWEEPS = 2


rotor_rate = 0.25
relaxation = 0.8
highest = lax.Precision.HIGHEST


def padded_2(block, sides, width):
    for axis, dim in sides:
        count = lax.axis_size(axis)
        forward = [(i, i + 1) for i in range(count - 1)]
        backward = [(target, source) for source, target in forward]
        low = lax.ppermute(
            lax.slice_in_dim(block, block.shape[dim] - width, None, axis=dim), axis, forward
        )
        high = lax.ppermute(lax.slice_in_dim(block, 0, width, axis=dim), axis, backward)
        block = jnp.concatenate([low, block, high], axis=dim)
    return block


def tables(period):
    angles = 2.0 * math.pi * jnp.arange(period, dtype=jnp.float32) / period
    half = period // 2
    frequency = jnp.arange(half + 1, dtype=jnp.float32)
    cosine = jnp.cos(frequency[:, None] * angles[None, :])
    sine_table = jnp.sin(frequency[:, None] * angles[None, :])
    spread = angles[:, None] - angles[None, :]
    orders = jnp.arange(1, half, dtype=jnp.float32)
    deriv = -(2.0 / period) * jnp.sum(
        orders[:, None, None] * jnp.sin(orders[:, None, None] * spread[None]), axis=0
    )
    weights = jnp.where((frequency == 0) | (frequency == half), 1.0 / period, 2.0 / period).astype(
        jnp.float32
    )
    return (angles, frequency, cosine, sine_table, deriv, weights)


def local(
    adjoint_start,
    source,
    jacobian_tiles,
    tile_columns,
    pseudo_time,
    control_terms,
    surface_rows,
    surface_weight,
    trim_inverse,
):
    inst_local, objectives, row_count = adjoint_start.shape
    tile_rows = jacobian_tiles.shape[-1]
    blocks = row_count // tile_rows
    angles, frequency, cosine, sine_table, deriv, weights = tables(INSTANCES)
    first_inst = lax.axis_index("inst") * inst_local
    own_angles = lax.dynamic_slice_in_dim(angles, first_inst, inst_local, 0)
    harmonics = jnp.stack([jnp.ones_like(own_angles), jnp.cos(own_angles), jnp.sin(own_angles)])
    columns = (tile_columns + 1).reshape(-1)
    own_deriv = lax.dynamic_slice_in_dim(deriv, first_inst, inst_local, 0)
    own_cosine = lax.dynamic_slice_in_dim(cosine, first_inst, inst_local, 1)
    own_sine = lax.dynamic_slice_in_dim(sine_table, first_inst, inst_local, 1)
    state_now = adjoint_start
    residual = adjoint_start
    for sweep_idx in range(SWEEPS):
        narrow = state_now.astype(jnp.bfloat16)
        padded = padded_2(narrow, (("span", 2),), tile_rows)
        stacked = padded.reshape(inst_local, objectives, blocks + 2, tile_rows)
        picked = jnp.take(stacked, columns, axis=2).reshape(
            inst_local, objectives, blocks, -1, tile_rows
        )
        result = jnp.einsum(
            "iobkr,ibkrs->iobs", picked, jacobian_tiles, preferred_element_type=jnp.float32
        )
        product = result.reshape(inst_local, objectives, row_count)
        surface = jnp.take(state_now, surface_rows, axis=2)
        whole_blade = lax.all_gather(surface, "span", axis=2, tiled=True)
        weighted = jnp.einsum("ci,ios->cos", harmonics, whole_blade, precision=highest)
        partial_sums = jnp.sum(weighted * surface_weight[:, None, :], axis=2)
        load_sums = lax.psum(partial_sums, "inst")
        multiplier = jnp.dot(trim_inverse, load_sums, precision=highest)
        control = jnp.einsum("cir,co->ior", control_terms, multiplier, precision=highest)
        base_term = source - product - control
        derived = jnp.einsum(
            "nm,mor->nor",
            own_deriv,
            lax.all_gather(state_now, "inst", axis=0, tiled=True),
            precision=highest,
        )
        residual = base_term + rotor_rate * derived
        shard_piece = lax.all_gather(residual, "inst", axis=0, tiled=True)
        cos_sum = jnp.einsum("fm,mor->for", cosine, shard_piece, precision=highest)
        sin_sum = jnp.einsum("fm,mor->for", sine_table, shard_piece, precision=highest)
        scaling = weights[:, None] / (pseudo_time[None, :] + rotor_rate * frequency[:, None])
        update = jnp.einsum(
            "fn,for->nor", own_cosine, cos_sum * scaling[:, None, :], precision=highest
        )
        update = update + jnp.einsum(
            "fn,for->nor", own_sine, sin_sum * scaling[:, None, :], precision=highest
        )
        state_now = state_now + relaxation * update
    return (state_now, residual)


def solution(mesh):
    return jax.shard_map(
        local,
        mesh=mesh,
        in_specs=(
            P("inst", None, "span"),
            P("inst", None, "span"),
            P("inst", "span", None, None, None),
            P("span", None),
            P("span"),
            P(None, "inst", "span"),
            P("span"),
            P(),
            P(),
        ),
        out_specs=(P("inst", None, "span"), P("inst", None, "span")),
        check_vma=False,
    )
```

profile of v0, /device:TPU:1, one launch (start us, length us, event | category | flops | bytes accessed | tf_op | source)
XLA Modules:
  0.0 306.7 jit_solution(7790529264269441897)
XLA Ops:
  9.0 3.3 %collective-permute-start.1 = (bf16[4,4,256]{2,1,0:T(4,128)(2,1)S(1)}, bf16[4,4,256]{2,1,0:T(4,128)(2,1)S(1)}, u32[]{:S(2)}, u32[]{:S(2)}) collective-permute-start(bf16[4,4,256]{2,1,0:T(4,128)(2,1)S(1)} %get-tuple-element.19), channel_id=1, source_target_pairs={{1,0},{2,1},{3,2},{4,3},{5,4},{6,5},{7,6},{8,7},{9,8},{10,9},{11,1... | collective-permute-start | bytes 24584 | tf_op jit(solution)/shard_map/ppermute | solution.py:25
  12.3 5.3 %copy.132 = f32[4,4,3072]{1,0,2:T(4,128)} copy(f32[4,4,3072]{2,1,0:T(4,128)} %param.13) | data formatting | bytes 393216 | tf_op args[0]
  17.6 4.8 %gather_fusion.1 = f32[768,4,4]{2,1,0:T(4,128)S(1)} fusion(f32[4,4,3072]{1,0,2:T(4,128)} %copy.132, s32[1024]{0:T(1024)S(1)} %pad_clamp_fusion), kind=kCustom, calls=%fused_computation.1.clone | custom fusion | bytes 101376 | tf_op jit(solution)/shard_map/jit(_take)/gather | solution.py:82
  22.4 2.8 select_bitcast_fusion.1
  25.9 42.0 %all_gather.18 = f32[4,4,12288]{2,1,0:T(4,128)S(1)} all-gather(f32[4,4,768]{2,1,0:T(4,128)S(1)} %copy.133), channel_id=1, replica_groups=mesh['inst'=8,'span'=16] {'span'}, dimensions={2}, use_global_device_ids=true | all-gather | bytes 835584 | tf_op jit(solution)/shard_map/all_gather | solution.py:83
  68.0 2.1 fusion.16
  72.0 15.3 %psum.14 = f32[3,4]{0,1:T(4,128)S(1)} all-reduce(f32[3,4]{0,1:T(4,128)S(1)} %fusion.16), channel_id=1, replica_groups=mesh['inst'=8,'span'=16] {'inst'}, use_global_device_ids=true, to_apply=%region_1.0 | all-reduce | flops 12 | bytes 96 | tf_op jit(solution)/shard_map/psum | solution.py:86
  89.9 8.9 %fusion.22 = f32[4,12,4,256,1]{3,2,4,1,0:T(4,128)S(1)} fusion(bf16[4,12,3,256,256]{4,3,2,1,0:T(8,128)(2,1)} %param.15, bf16[4,4,12,3,256]{4,1,0,3,2:T(4,128)(2,1)S(1)} %bitcast.92), kind=kOutput, calls=%fused_computation.40 | convolution fusion | flops 75497472 | bytes 19365888 | tf_op jit(solution)/shard_map/iobkr,ibkrs->iobs/dot_general | solution.py:78
  98.8 3.1 %fusion.10 = f32[4,4,3072]{2,0,1:T(4,128)S(1)} fusion(f32[32,4,3072]{2,1,0:T(4,128)} %all-gather.5.cloned.1.call-done, f32[32,32]{1,0:T(8,128)S(1)} %multiply_reduce_fusion, s32[]{:T(128)S(6)} %select_n.28), kind=kOutput, calls=%fused_computation.24 | convolution fusion | flops 18874496 | bytes 1771524 | tf_op jit(solution)/shard_map/nm,mor->nor/dot_general | solution.py:90
  103.7 39.3 %all-gather.7.cloned.1.call-done = f32[32,4,3072]{2,1,0:T(4,128)} async-done(((f32[4,4,3072]{2,1,0:T(4,128)}), f32[32,4,3072]{2,1,0:T(4,128)}) %all-gather.7.cloned.1.call-update) | async-done | bytes 1572880 | tf_op jit(solution)/shard_map/all_gather | solution.py:97
  143.1 3.5 %convolution_multiply_fusion.5 = f32[17,4,3072]{2,0,1:T(8,128)S(1)} fusion(f32[32,4,3072]{2,1,0:T(4,128)} %all-gather.7.cloned.1.call-done, f32[17,3072]{1,0:T(8,128)S(1)} %add_divide_fusion, f32[32]{0:T(128)S(1)} %iota_multiply_fusion.2), kind=kOutput, calls=%fused_computation.9 | convolution fusion | flops 80425504 | bytes 2617472 | tf_op jit(solution)/shard_map/fm,mor->for/dot_general | solution.py:98
  147.4 2.0 convolution_multiply_fusion.4
  150.4 4.6 %copy.147 = f32[4,4,3072]{1,0,2:T(4,128)} copy(f32[4,4,3072]{2,0,1:T(4,128)S(1)} %get-tuple-element.25) | data formatting | bytes 393216 | tf_op jit(solution)/shard_map/add | solution.py:107
  155.8 5.8 %gather_fusion.3 = f32[768,4,4]{2,1,0:T(4,128)} fusion(f32[4,4,3072]{1,0,2:T(4,128)} %copy.147, s32[1024]{0:T(1024)S(1)} %pad_clamp_fusion), kind=kCustom, calls=%fused_computation.3.clone | custom fusion | bytes 101376 | tf_op jit(solution)/shard_map/jit(_take)/gather | solution.py:82
  161.7 4.1 %select_bitcast_fusion = f32[4,4,768]{1,0,2:T(4,128)S(1)} fusion(f32[768,4,4]{2,1,0:T(4,128)} %gather_fusion.3, pred[768]{0:T(1024)(128)(4,1)S(1)} %compare_and_fusion), kind=kLoop, calls=%fused_computation.26 | loop fusion | flops 12288 | bytes 99072 | tf_op jit(solution)/shard_map/jit(_take)/select_n | solution.py:82
  166.4 44.7 %all_gather.21 = f32[4,4,12288]{2,1,0:T(4,128)S(1)} all-gather(f32[4,4,768]{2,1,0:T(4,128)S(1)} %copy.148), channel_id=1, replica_groups=mesh['inst'=8,'span'=16] {'span'}, dimensions={2}, use_global_device_ids=true | all-gather | bytes 835584 | tf_op jit(solution)/shard_map/all_gather | solution.py:83
  211.2 2.1 fusion.17
  213.2 14.1 %psum.15 = f32[3,4]{0,1:T(4,128)S(1)} all-reduce(f32[3,4]{0,1:T(4,128)S(1)} %fusion.17), channel_id=1, replica_groups=mesh['inst'=8,'span'=16] {'inst'}, use_global_device_ids=true, to_apply=%region_4.7 | all-reduce | flops 12 | bytes 96 | tf_op jit(solution)/shard_map/psum | solution.py:86
  227.3 5.7 %collective-permute-start.3 = (bf16[4,4,256]{2,0,1:T(4,128)(2,1)S(1)}, bf16[4,4,256]{2,0,1:T(4,128)(2,1)S(1)}, u32[]{:S(2)}, u32[]{:S(2)}) collective-permute-start(bf16[4,4,256]{2,0,1:T(4,128)(2,1)S(1)} %get-tuple-element.17), channel_id=1, source_target_pairs={{1,0},{2,1},{3,2},{4,3},{5,4},{6,5},{7,6},{8,7},{9,8},{10,9},{11,1... | collective-permute-start | bytes 24584 | tf_op jit(solution)/shard_map/ppermute | solution.py:25
  233.1 2.1 collective-permute-start.2
  237.4 8.9 %fusion.20 = f32[4,12,4,256,1]{3,2,4,1,0:T(4,128)S(1)} fusion(bf16[4,12,3,256,256]{4,3,2,1,0:T(8,128)(2,1)} %param.15, bf16[4,4,12,3,256]{4,1,0,3,2:T(4,128)(2,1)S(1)} %bitcast.91), kind=kOutput, calls=%fused_computation.38 | convolution fusion | flops 75497472 | bytes 19365888 | tf_op jit(solution)/shard_map/iobkr,ibkrs->iobs/dot_general | solution.py:78
  246.4 3.1 fusion.8
  250.8 41.4 %all-gather.11.cloned.1.call-done = f32[32,4,3072]{2,1,0:T(4,128)} async-done(((f32[4,4,3072]{2,1,0:T(4,128)}), f32[32,4,3072]{2,1,0:T(4,128)}) %all-gather.11.cloned.1.call-update) | async-done | bytes 1572880 | tf_op jit(solution)/shard_map/all_gather | solution.py:97
  292.2 3.5 %convolution_multiply_fusion.3 = f32[17,4,3072]{2,0,1:T(8,128)S(1)} fusion(f32[32,4,3072]{2,1,0:T(4,128)} %all-gather.11.cloned.1.call-done, f32[17,3072]{1,0:T(8,128)S(1)} %add_divide_fusion, f32[32]{0:T(128)S(1)} %iota_multiply_fusion.2), kind=kOutput, calls=%fused_computation.7 | convolution fusion | flops 80425504 | bytes 2617472 | tf_op jit(solution)/shard_map/fm,mor->for/dot_general | solution.py:98
  (77 shorter events, 20.0 us)
Async XLA Ops:
  7.2 94.8 %copy-start = (f32[3,4,3072]{2,1,0:T(4,128)S(1)}, f32[3,4,3072]{2,1,0:T(4,128)}, u32[]{:S(2)}) copy-start(f32[3,4,3072]{2,1,0:T(4,128)} %param.18) | copy-start | bytes 442372
  7.2 91.6 %all-gather.5.cloned.1.call-start = ((), (), s32[]{:S(2)}) async-start(), calls=%async_computation | async-start | bytes 1769472 | tf_op jit(solution)/shard_map/all_gather | solution.py:93
  7.9 135.1 %all-gather.7.cloned.1.call-start = ((), (), s32[]{:S(2)}) async-start(), calls=%async_computation.1 | async-start | bytes 1769472 | tf_op jit(solution)/shard_map/all_gather | solution.py:97
  8.9 8.6 %copy-start.5 = (s32[768]{0:T(1024)S(1)}, s32[768]{0:T(1024)}, u32[]{:S(2)}) copy-start(s32[768]{0:T(1024)} %param.19) | copy-start | bytes 9220
  9.0 79.8 %collective-permute-start.1 = (bf16[4,4,256]{2,1,0:T(4,128)(2,1)S(1)}, bf16[4,4,256]{2,1,0:T(4,128)(2,1)S(1)}, u32[]{:S(2)}, u32[]{:S(2)}) collective-permute-start(bf16[4,4,256]{2,1,0:T(4,128)(2,1)S(1)} %get-tuple-element.19), channel_id=1, source_target_pairs={{1,0},{2,1},{3,2},{4,3},{5,4},{6,5},{7,6},{8,7},{9,8},{10,9},{11,1... | collective-permute-start | bytes 24584 | tf_op jit(solution)/shard_map/ppermute | solution.py:25
  25.2 42.9 %copy-start.9 = (f32[3,12288]{1,0:T(4,128)S(1)}, f32[3,12288]{1,0:T(4,128)}, u32[]{:S(2)}) copy-start(f32[3,12288]{1,0:T(4,128)} %param.20) | copy-start | bytes 442372
  25.2 62.2 %copy-start.8 = (s32[12,3]{0,1:T(4,128)S(1)}, s32[12,3]{0,1:T(4,128)}, u32[]{:S(2)}) copy-start(s32[12,3]{0,1:T(4,128)} %param.16) | copy-start | bytes 436
  25.2 62.4 %copy-start.7 = (f32[3,3]{1,0:T(4,128)S(1)}, f32[3,3]{1,0:T(4,128)}, u32[]{:S(2)}) copy-start(f32[3,3]{1,0:T(4,128)} %param.21) | copy-start | bytes 112
  70.1 18.6 %collective-permute-start = (bf16[4,4,256]{2,1,0:T(4,128)(2,1)S(1)}, bf16[4,4,256]{2,1,0:T(4,128)(2,1)S(1)}, u32[]{:S(2)}, u32[]{:S(2)}) collective-permute-start(bf16[4,4,256]{2,1,0:T(4,128)(2,1)S(1)} %get-tuple-element.18), channel_id=1, source_target_pairs={{0,1},{1,2},{2,3},{3,4},{4,5},{5,6},{6,7},{7,8},{8,9},{9,10},{10,1... | collective-permute-start | bytes 24584 | tf_op jit(solution)/shard_map/ppermute | solution.py:22
  98.8 3.1 %copy-start.4 = (f32[4,4,3072]{2,1,0:T(4,128)S(1)}, f32[4,4,3072]{2,1,0:T(4,128)}, u32[]{:S(2)}) copy-start(f32[4,4,3072]{2,1,0:T(4,128)} %param.14) | copy-start | bytes 589828
  98.8 4.8 %copy-start.6 = (f32[3072]{0:T(1024)S(1)}, f32[3072]{0:T(1024)}, u32[]{:S(2)}) copy-start(f32[3072]{0:T(1024)} %param.17) | copy-start | bytes 36868
  103.3 143.1 %all-gather.9.cloned.1.call-start = ((), (), s32[]{:S(2)}) async-start(), calls=%async_computation.2 | async-start | bytes 1769472 | tf_op jit(solution)/shard_map/all_gather | solution.py:93
  143.0 4.3 %copy-start.1 = (f32[32,4,3072]{2,1,0:T(4,128)S(1)}, f32[32,4,3072]{2,1,0:T(4,128)}, u32[]{:S(2)}) copy-start(f32[32,4,3072]{2,1,0:T(4,128)} %all-gather.7.cloned.1.call-done) | copy-start | bytes 4718596
  147.4 2.0 copy-start.3
  161.6 130.6 %all-gather.11.cloned.1.call-start = ((), (), s32[]{:S(2)}) async-start(), calls=%async_computation.3 | async-start | bytes 1769472 | tf_op jit(solution)/shard_map/all_gather | solution.py:97
  227.3 8.0 %collective-permute-start.3 = (bf16[4,4,256]{2,0,1:T(4,128)(2,1)S(1)}, bf16[4,4,256]{2,0,1:T(4,128)(2,1)S(1)}, u32[]{:S(2)}, u32[]{:S(2)}) collective-permute-start(bf16[4,4,256]{2,0,1:T(4,128)(2,1)S(1)} %get-tuple-element.17), channel_id=1, source_target_pairs={{1,0},{2,1},{3,2},{4,3},{5,4},{6,5},{7,6},{8,7},{9,8},{10,9},{11,1... | collective-permute-start | bytes 24584 | tf_op jit(solution)/shard_map/ppermute | solution.py:25
  233.1 3.1 collective-permute-start.2
  292.2 4.3 %copy-start.2 = (f32[32,4,3072]{2,1,0:T(4,128)S(1)}, f32[32,4,3072]{2,1,0:T(4,128)}, u32[]{:S(2)}) copy-start(f32[32,4,3072]{2,1,0:T(4,128)} %all-gather.11.cloned.1.call-done) | copy-start | bytes 4718596
Sparse Core Ops, SparseCore 0:
  9.7 51.2 all-gather.4
  103.4 39.5 all-gather.6
  161.7 49.6 all-gather.8
  250.9 41.2 all-gather.10
where the time goes:
time: 309 us; the launch traced here: 307 us
  blocking collectives  116 us (38%)
  waiting for transfers between devices  82.3 us (27%)
  matrix products  45.5 us (15%)
  local copies, waits for them, and re-layouts  25.6 us (8%)
  between operations  14.2 us (5%)
  starting transfers between devices  13.5 us (4%)
  other arithmetic  9.59 us (3%)
    all_gather x2, blocking collectives, local(): whole_blade = lax.all_gather(surface, 'span', axis=2, tiled=True)  86.8 us
    all_gather x2, waiting for transfers between devices, local(): shard_piece = lax.all_gather(residual, 'inst', axis=0, tiled=True)  80.7 us
    psum x2, blocking collectives, local(): load_sums = lax.psum(partial_sums, 'inst')  29.4 us
    dot_general x2, matrix products, local(): jnp.einsum('iobkr,ibkrs->iobs', picked, jacobian_tiles, preferred_element...  17.9 us
    gather x2, local copies, waits for them, and re-layouts, local(): surface = jnp.take(state_now, surface_rows, axis=2)  10.6 us
    ppermute x2, starting transfers between devices, padded_2(): lax.ppermute(lax.slice_in_dim(block, 0, width, axis=dim), axis, backward)  9.06 us
    dot_general x2, matrix products, local(): cos_sum = jnp.einsum('fm,mor->for', cosine, shard_piece, precision=highest)  6.9 us
    select_n x3, other arithmetic, local(): surface = jnp.take(state_now, surface_rows, axis=2)  6.86 us
  transfers between devices with their start and end apart: 8, of which 3 were waited for; matrix products, arithmetic and copies ran while one was open for 15% of the time, Pallas kernels for 0%

commit v1 on v0

v1 whole, which is shorter than its diff:
```python
import math

import jax
import jax.numpy as jnp
import ml_dtypes
import numpy as np
from jax import lax
from jax.experimental import pallas as pl
from jax.experimental.pallas import tpu as pltpu
from jax.sharding import PartitionSpec as P

MESH = pl.DeviceIdType.MESH
F32 = jnp.float32
BF16 = jnp.bfloat16

INST = 32
PEERS = 8
OWN = 4
NOBJ = 4
ROWS = 3072
NB = 12
K = 3
TILE = 256
S_DEV = 768
RATE = 0.25
RELAX = 0.8


def split_const(a):
    hi = a.astype(ml_dtypes.bfloat16)
    lo = (a - hi.astype(np.float64)).astype(ml_dtypes.bfloat16)
    return np.concatenate([hi, hi, lo], axis=-1)


def constants():
    theta = 2.0 * math.pi * np.arange(INST) / INST
    half = INST // 2
    trans = np.concatenate(
        [
            np.cos(np.arange(half + 1)[:, None] * theta[None, :]),
            np.sin(np.arange(1, half)[:, None] * theta[None, :]),
        ]
    )
    spread = theta[:, None] - theta[None, :]
    orders = np.arange(1, half)[:, None, None]
    deriv = -(2.0 / INST) * np.sum(orders * np.sin(orders * spread[None]), axis=0)
    eye = np.eye(NOBJ)
    forward = np.kron(trans, eye)
    back = np.kron(trans.T, eye)
    forward_deriv = RATE * np.kron(trans @ deriv, eye)
    own_deriv = RATE * np.kron(deriv, eye)
    mats = np.stack([split_const(m) for m in (forward, back, forward_deriv, own_deriv)])
    angle = np.repeat(theta, NOBJ)
    harm = np.stack([np.cos(angle), np.sin(angle)]).astype(np.float32)
    harm = np.ascontiguousarray(np.broadcast_to(harm[:, :, None], (2, 128, 128)))
    return mats, harm


def exact_dot(mat, x):
    hi = x.astype(BF16)
    lo = (x - hi.astype(F32)).astype(BF16)
    return jnp.dot(mat, jnp.concatenate([hi, lo, hi], axis=0), preferred_element_type=F32)


def kernel(
    n_span,
    cols_ref,
    tinv_ref,
    state_hbm,
    source_hbm,
    jac_hbm,
    pt_hbm,
    ct_hbm,
    rows_hbm,
    sw_hbm,
    mats_hbm,
    harm_hbm,
    adj_hbm,
    res_hbm,
    jbuf,
    st_v,
    src_v,
    ct_v,
    pt_v,
    rows_v,
    sw_v,
    mats_v,
    harm_v,
    out_a,
    out_r,
    s0,
    n0,
    n1,
    nf,
    w_v,
    base1,
    base2,
    xs,
    xb1,
    xb2,
    scal,
    yd,
    ns,
    ds_,
    dr,
    as_,
    ar,
    r1s,
    r1r,
    r2s,
    r2r,
    j_sem,
    l_sem,
    st_send,
    st_recv,
    h0_send,
    h0_recv,
    b_send,
    b_recv,
    n_send,
    n_recv,
    h1_send,
    h1_recv,
    d_send,
    d_recv,
    a_send,
    a_recv,
    r1_send,
    r1_recv,
    r2_send,
    r2_recv,
):
    me = lax.axis_index("inst")
    sp = lax.axis_index("span")
    last = n_span - 1

    local_in = [
        (state_hbm, st_v),
        (rows_hbm, rows_v),
        (sw_hbm.at[:, pl.ds(pl.multiple_of(sp * S_DEV, S_DEV), S_DEV)], sw_v),
        (harm_hbm, harm_v),
        (source_hbm, src_v),
        (ct_hbm, ct_v),
        (pt_hbm, pt_v),
        (mats_hbm, mats_v),
    ]
    loads = [pltpu.make_async_copy(a, b, l_sem.at[n]) for n, (a, b) in enumerate(local_in)]
    for c in loads:
        c.start()

    def jac_copy(b):
        return pltpu.make_async_copy(jac_hbm.at[:, b], jbuf.at[b], j_sem.at[b])

    @pl.loop(0, NB)
    def _(b):
        jac_copy(b).start()

    zero2 = jnp.zeros((2, 16, 128), BF16)
    n1[0, 6:8] = zero2
    n1[4, 0:2] = zero2
    for column in (0, NB + 1):
        n0[column] = jnp.zeros((16, TILE), BF16)

    barrier = pltpu.get_barrier_semaphore()

    def signal(i, s):
        pl.semaphore_signal(barrier, inc=1, device_id=(i, s), device_id_type=MESH)

    def peers(fn):
        @pl.loop(1, PEERS)
        def _(d):
            fn(lax.rem(me + d, PEERS))

    def spans(fn):
        @pl.loop(1, n_span)
        def _(d):
            fn(lax.rem(sp + d, n_span))

    peers(lambda p: signal(p, sp))
    spans(lambda q: signal(me, q))

    has_low = sp > 0
    has_high = sp < last
    def at_low(fn):
        @pl.when(has_low)
        def _():
            @pl.when(me < 2)
            def _():
                pl.loop(0, PEERS)(fn)

    def at_high(fn):
        @pl.when(has_high)
        def _():
            @pl.when(me >= PEERS - 2)
            def _():
                pl.loop(0, PEERS)(fn)

    def around(p):
        signal(p, lax.rem(sp + 1, n_span))
        signal(p, lax.rem(sp + n_span - 1, n_span))

    peers(around)

    loads[0].wait()
    flat = jnp.concatenate([st_v[i] for i in range(OWN)], axis=0)
    for q in range(24):
        piece = flat[:, q * 128 : (q + 1) * 128]
        s0[q // 8, q % 8] = piece
    for b in range(NB):
        n0[b + 1] = flat[:, b * TILE : (b + 1) * TILE].astype(BF16)

    pl.semaphore_wait(barrier, 3 * (PEERS - 1) + n_span - 1)

    def to(src, dst, send, recv, i, s):
        return pltpu.make_async_remote_copy(
            src_ref=src, dst_ref=dst, send_sem=send, recv_sem=recv, device_id=(i, s), device_id_type=MESH
        )

    def halo0_low():
        return to(n0.at[1], n0.at[NB + 1], h0_send.at[0], h0_recv.at[0], me, sp - 1)

    def halo0_high():
        return to(n0.at[NB], n0.at[0], h0_send.at[1], h0_recv.at[1], me, sp + 1)

    def state_out(p):
        return to(s0.at[:, p], xs.at[me], st_send.at[p], st_recv.at[me], p, sp)

    def base_out(k, t, p):
        src, dst = (base1, xb1) if k == 0 else (base2, xb2)
        return to(src.at[t, p], dst.at[me, t], b_send.at[k, t, p], b_recv.at[k, t, me], p, sp)

    def narrow_out(p):
        return to(ns.at[p], n1.at[pl.ds(1, 3), me], n_send.at[p], n_recv.at[me], p, sp)

    def halo1_low(p):
        return to(ns.at[p, 0], n1.at[4, me], h1_send.at[0, p], h1_recv.at[me], p, sp - 1)

    def halo1_high(p):
        return to(ns.at[p, 2], n1.at[0, me], h1_send.at[1, p], h1_recv.at[me], p, sp + 1)

    def deriv_out(p):
        return to(ds_.at[p], dr.at[:, me], d_send.at[p], d_recv.at[me], p, sp)

    def adj_out(p):
        return to(as_.at[p], ar.at[:, me], a_send.at[p], a_recv.at[me], p, sp)

    def sum1_out(k, q):
        return to(r1s.at[k], r1r.at[k, sp], r1_send.at[k, q], r1_recv.at[k, sp], me, q)

    def sum2_out(k, p):
        return to(r2s.at[k], r2r.at[k, me], r2_send.at[k, p], r2_recv.at[k, me], p, sp)

    def arrived(dst, sem):
        pltpu.make_async_copy(dst, dst, sem).wait()

    @pl.when(has_low)
    def _():
        halo0_low().start()

    @pl.when(has_high)
    def _():
        halo0_high().start()

    loads[1].wait()
    loads[2].wait()
    rows = jnp.concatenate([rows_v[q : q + 1, :] for q in range(6)], axis=1)
    high, low = lax.div(rows, 128), lax.rem(rows, 128)
    tiles24 = lax.broadcasted_iota(jnp.int32, (24, S_DEV), 0)
    hit = jnp.broadcast_to(high, (24, S_DEV)) == tiles24
    spread = jnp.concatenate(
        [jnp.where(hit, jnp.broadcast_to(sw_v[c : c + 1, :], (24, S_DEV)), 0.0) for c in range(3)], axis=0
    )
    spread_hi = spread.astype(BF16)
    spread_lo = (spread - spread_hi.astype(F32)).astype(BF16)
    lane_hit = jnp.broadcast_to(low, (128, S_DEV)) == lax.broadcasted_iota(jnp.int32, (128, S_DEV), 0)
    lane_hit = jnp.where(lane_hit, 1.0, 0.0).astype(BF16)
    nt = (((1,), (1,)), ((), ()))
    w_v[...] = lax.dot_general(spread_hi, lane_hit, nt, preferred_element_type=F32) + lax.dot_general(
        spread_lo, lane_hit, nt, preferred_element_type=F32
    )

    lane8 = lax.broadcasted_iota(jnp.int32, (8, 128), 1)
    row8 = lax.rem(lax.broadcasted_iota(jnp.int32, (8, 128), 0), NOBJ)

    def load_row(accs):
        total = jnp.zeros((8, 128), F32)
        for c in range(3):
            col = jnp.sum(accs[c], axis=1, keepdims=True)
            total = total + jnp.where(lane8 == c * NOBJ + row8, jnp.broadcast_to(col, (8, 128)), 0.0)
        return jnp.sum(total, axis=0, keepdims=True)

    loads[3].wait()
    accs = []
    for c in range(3):
        acc = jnp.zeros((16, 128), F32)
        for q in range(24):
            acc = acc + s0[q // 8, q % 8] * jnp.broadcast_to(w_v[c * 24 + q : c * 24 + q + 1, :], (16, 128))
        if c > 0:
            acc = acc * harm_v[c - 1, pl.ds(pl.multiple_of(me * 16, 16), 16), :]
        accs.append(acc[0:8] + acc[8:16])

    def start_sum(k, row):
        r1s[k] = row
        r1r[k, pl.ds(sp, 1)] = row.reshape(1, 1, 128)
        spans(lambda q: sum1_out(k, q).start())

    start_sum(0, load_row(accs))
    peers(lambda p: state_out(p).start())
    xs[pl.ds(me, 1)] = s0[:, pl.ds(me, 1)].reshape(1, 3, 16, 128)

    def middle_sum(k):
        spans(lambda q: arrived(r1r.at[k, q], r1_recv.at[k, q]))
        row = jnp.sum(r1r[k], axis=0)
        r2s[k] = row
        r2r[k, pl.ds(me, 1)] = row.reshape(1, 1, 128)
        peers(lambda p: sum2_out(k, p).start())

    lane16 = lax.broadcasted_iota(jnp.int32, (16, 128), 1)
    row16 = lax.rem(lax.broadcasted_iota(jnp.int32, (16, 128), 0), NOBJ)

    def multiplier(k):
        peers(lambda p: arrived(r2r.at[k, p], r2_recv.at[k, p]))
        row = jnp.broadcast_to(jnp.sum(r2r[k], axis=0), (16, 128))
        out = []
        for c in range(3):
            mask = jnp.zeros((16, 128), F32)
            for d in range(3):
                mask = jnp.where(lane16 == d * NOBJ + row16, tinv_ref[c, d], mask)
            col = jnp.sum(row * mask, axis=1, keepdims=True)
            out.append(jnp.broadcast_to(col, (16, 128)))
        return out

    inst_row = lax.div(lax.broadcasted_iota(jnp.int32, (16, TILE), 0), NOBJ)
    masks = [jnp.where(inst_row == i, 1.0, 0.0).astype(BF16) for i in range(OWN)]

    def product(b, narrow, base):
        acc = jnp.zeros((16, TILE), F32)
        for k in range(K):
            block = narrow[cols_ref[b, k] + 1]
            for i in range(OWN):
                acc = acc + jnp.dot(block * masks[i], jbuf[b, i, k], preferred_element_type=F32)
        for half in range(2):
            q = 2 * b + half
            base[lax.div(q, 8), lax.rem(q, 8)] = acc[:, half * 128 : (half + 1) * 128]

    row8i = lax.div(lax.broadcasted_iota(jnp.int32, (8, 128), 0), NOBJ)

    def finish(q, k, base, mult):
        lanes = pl.ds(pl.multiple_of(q * 128, 128), 128)
        t, p = lax.div(q, 8), lax.rem(q, 8)
        value = jnp.concatenate([src_v[i, :, lanes] for i in range(OWN)], axis=0) - base[t, p]
        for c in range(3):
            parts = []
            for h in range(2):
                first = jnp.broadcast_to(ct_v[c, 2 * h : 2 * h + 1, lanes], (8, 128))
                second = jnp.broadcast_to(ct_v[c, 2 * h + 1 : 2 * h + 2, lanes], (8, 128))
                parts.append(jnp.where(row8i == 0, first, second))
            value = value - jnp.concatenate(parts, axis=0) * mult[c]
        base[t, p] = value

        @pl.when(p != me)
        def _():
            base_out(k, t, p).start()

        @pl.when(p == me)
        def _():
            (xb1 if k == 0 else xb2)[me, t] = value

    def sweep_products(k, narrow, base, between):
        def one(b):
            if k == 0:
                jac_copy(b).wait()
            product(b, narrow, base)

        pl.loop(0, 4)(one)
        middle_sum(k)
        pl.loop(4, 8)(one)
        between()
        mult = multiplier(k)
        pl.loop(0, 16)(lambda q: finish(q, k, base, mult))

        @pl.loop(8, NB)
        def _(b):
            one(b)
            finish(2 * b, k, base, mult)
            finish(2 * b + 1, k, base, mult)

    def wide(ref):
        return jnp.concatenate([ref[:, t].reshape(128, 128) for t in range(3)], axis=1)

    @pl.when(has_high)
    def _():
        arrived(n0.at[NB + 1], h0_recv.at[0])

    @pl.when(has_low)
    def _():
        arrived(n0.at[0], h0_recv.at[1])

    def first_between():
        for c in loads[4:]:
            c.wait()
        order = lax.div(lax.broadcasted_iota(jnp.int32, (128, 128), 0), NOBJ)
        freq = jnp.where(order > INST // 2, order - INST // 2, order)
        ends = jnp.logical_or(freq == 0, freq == INST // 2)
        weight = jnp.where(ends, RELAX / INST, 2.0 * RELAX / INST)
        offset = RATE * freq.astype(F32)
        for t in range(3):
            pt = jnp.broadcast_to(pt_v[t, pl.ds(me, 1), :], (128, 128))
            scal[:, t * 128 : (t + 1) * 128] = weight / (pt + offset)
        peers(lambda p: arrived(xs.at[p], st_recv.at[p]))
        yd[...] = exact_dot(mats_v[2], wide(xs))

    sweep_products(0, n0, base1, first_between)

    def wait_base(k):
        @pl.loop(0, 3)
        def _(t):
            peers(lambda p: arrived((xb1 if k == 0 else xb2).at[p, t], b_recv.at[k, t, p]))

    wait_base(0)
    spectrum = exact_dot(mats_v[0], wide(xb1)) + yd[...]
    state1 = wide(xs) + exact_dot(mats_v[1], spectrum * scal[...])
    for t in range(3):
        piece = state1[:, t * 128 : (t + 1) * 128]
        xs[:, t] = piece.reshape(PEERS, 16, 128)
        ns[:, t] = piece.astype(BF16).reshape(PEERS, 16, 128)
    peers(lambda p: narrow_out(p).start())

    at_low(lambda p: halo1_low(p).start())
    at_high(lambda p: halo1_high(p).start())

    n1[pl.ds(1, 3), pl.ds(me, 1)] = ns[pl.ds(me, 1)].reshape(3, 1, 16, 128)

    accs = []
    for c in range(3):
        acc = jnp.zeros((128, 128), F32)
        for t in range(3):
            weight = w_v[pl.ds(c * 24 + t * 8 + me, 1), :]
            acc = acc + state1[:, t * 128 : (t + 1) * 128] * jnp.broadcast_to(weight, (128, 128))
        if c > 0:
            acc = acc * harm_v[c - 1]
        accs.append(jnp.sum(acc.reshape(16, 8, 128), axis=0))
    start_sum(1, load_row(accs))

    yd[...] = exact_dot(mats_v[2], state1)
    derived = exact_dot(mats_v[3], state1)
    for t in range(3):
        ds_[:, t] = derived[:, t * 128 : (t + 1) * 128].reshape(PEERS, 16, 128)
    peers(lambda p: deriv_out(p).start())
    dr[:, pl.ds(me, 1)] = ds_[pl.ds(me, 1)].reshape(3, 1, 16, 128)

    peers(lambda p: arrived(n1.at[pl.ds(1, 3), p], n_recv.at[p]))

    @pl.when(has_high)
    def _():
        pl.loop(0, 2)(lambda p: arrived(n1.at[4, p], h1_recv.at[p]))

    @pl.when(has_low)
    def _():
        pl.loop(PEERS - 2, PEERS)(lambda p: arrived(n1.at[0, p], h1_recv.at[p]))

    for column in range(NB + 2):
        slot = 2 * column + 6
        left, right = n1[slot // 8, slot % 8], n1[slot // 8, slot % 8 + 1]
        nf[column] = jnp.concatenate([left, right], axis=1)

    sweep_products(1, nf, base2, lambda: None)

    wait_base(1)
    spectrum = exact_dot(mats_v[0], wide(xb2)) + yd[...]
    final = wide(xs) + exact_dot(mats_v[1], spectrum * scal[...])
    for t in range(3):
        as_[:, t] = final[:, t * 128 : (t + 1) * 128].reshape(PEERS, 16, 128)
    peers(lambda p: adj_out(p).start())
    ar[:, pl.ds(me, 1)] = as_[pl.ds(me, 1)].reshape(3, 1, 16, 128)

    def put(out, fn):
        for q in range(24):
            value = fn(q // 8, q % 8)
            for i in range(OWN):
                out[i, :, q * 128 : (q + 1) * 128] = value[i * NOBJ : (i + 1) * NOBJ, :]

    peers(lambda p: arrived(dr.at[:, p], d_recv.at[p]))
    put(out_r, lambda t, p: base2[t, p] + dr[t, p])
    write_r = pltpu.make_async_copy(out_r, res_hbm, l_sem.at[0])
    write_r.start()
    peers(lambda p: arrived(ar.at[:, p], a_recv.at[p]))
    put(out_a, lambda t, p: ar[t, p])
    write_a = pltpu.make_async_copy(out_a, adj_hbm, l_sem.at[1])
    write_a.start()

    @pl.when(has_low)
    def _():
        halo0_low().wait_send()

    @pl.when(has_high)
    def _():
        halo0_high().wait_send()

    at_low(lambda p: halo1_low(p).wait_send())
    at_high(lambda p: halo1_high(p).wait_send())

    def drain(p):
        state_out(p).wait_send()
        narrow_out(p).wait_send()
        deriv_out(p).wait_send()
        adj_out(p).wait_send()
        for k in range(2):
            sum2_out(k, p).wait_send()
            for t in range(3):
                base_out(k, t, p).wait_send()

    peers(drain)

    def drain_span(q):
        for k in range(2):
            sum1_out(k, q).wait_send()

    spans(drain_span)
    write_r.wait()
    write_a.wait()


def solution(mesh):
    n_span = mesh.shape["span"]
    mats, harm = constants()

    def local(
        adjoint_start,
        source,
        jacobian_tiles,
        tile_columns,
        pseudo_time,
        control_terms,
        surface_rows,
        surface_weight,
        trim_inverse,
    ):
        any_spec = pl.BlockSpec(memory_space=pl.ANY)
        smem = pl.BlockSpec(memory_space=pltpu.SMEM)
        dma = pltpu.SemaphoreType.DMA
        vm = pltpu.VMEM
        out = jax.ShapeDtypeStruct((OWN, NOBJ, ROWS), F32)
        return pl.pallas_call(
            lambda *refs: kernel(n_span, *refs),
            out_shape=(out, out),
            in_specs=[smem, smem] + [any_spec] * 9,
            out_specs=(any_spec, any_spec),
            scratch_shapes=[
                vm((NB, OWN, K, TILE, TILE), BF16),
                vm((OWN, NOBJ, ROWS), F32),
                vm((OWN, NOBJ, ROWS), F32),
                vm((3, OWN, ROWS), F32),
                vm((3, 8, 128), F32),
                vm((6, 128), jnp.int32),
                vm((3, S_DEV), F32),
                vm((4, 128, 384), BF16),
                vm((2, 128, 128), F32),
                vm((OWN, NOBJ, ROWS), F32),
                vm((OWN, NOBJ, ROWS), F32),
                vm((3, 8, 16, 128), F32),
                vm((NB + 2, 16, TILE), BF16),
                vm((5, 8, 16, 128), BF16),
                vm((NB + 2, 16, TILE), BF16),
                vm((72, 128), F32),
                vm((3, 8, 16, 128), F32),
                vm((3, 8, 16, 128), F32),
                vm((8, 3, 16, 128), F32),
                vm((8, 3, 16, 128), F32),
                vm((8, 3, 16, 128), F32),
                vm((128, 384), F32),
                vm((128, 384), F32),
                vm((8, 3, 16, 128), BF16),
                vm((8, 3, 16, 128), F32),
                vm((3, 8, 16, 128), F32),
                vm((8, 3, 16, 128), F32),
                vm((3, 8, 16, 128), F32),
                vm((2, 1, 128), F32),
                vm((2, n_span, 1, 128), F32),
                vm((2, 1, 128), F32),
                vm((2, PEERS, 1, 128), F32),
                dma((NB,)),
                dma((8,)),
                dma((8,)),
                dma((8,)),
                dma((2,)),
                dma((2,)),
                dma((2, 3, 8)),
                dma((2, 3, 8)),
                dma((8,)),
                dma((8,)),
                dma((2, 8)),
                dma((8,)),
                dma((8,)),
                dma((8,)),
                dma((8,)),
                dma((8,)),
                dma((2, n_span)),
                dma((2, n_span)),
                dma((2, 8)),
                dma((2, 8)),
            ],
            compiler_params=pltpu.CompilerParams(
                collective_id=0, has_side_effects=True, vmem_limit_bytes=40 * 1024 * 1024
            ),
        )(
            tile_columns,
            trim_inverse,
            adjoint_start,
            source,
            jacobian_tiles,
            pseudo_time.reshape(3, 8, 128),
            control_terms,
            surface_rows.reshape(6, 128),
            surface_weight,
            jnp.asarray(mats),
            jnp.asarray(harm),
        )

    return jax.shard_map(
        local,
        mesh=mesh,
        in_specs=(
            P("inst", None, "span"),
            P("inst", None, "span"),
            P("inst", "span", None, None, None),
            P("span", None),
            P("span"),
            P(None, "inst", "span"),
            P("span"),
            P(),
            P(),
        ),
        out_specs=(P("inst", None, "span"), P("inst", None, "span")),
        check_vma=False,
    )
```

time: 309 us -> 59.5 us (0.19)
  the two profiles are of different devices: /device:TPU:1 before, /device:TPU:0 now
where the time goes in v1:
time: 59.5 us; the launch traced here: 59.1 us
  Pallas kernels  48.7 us (82%)
  local copies, waits for them, and re-layouts  9.79 us (16%)
  between operations  0.65 us (1%)
    pallas_call x1, Pallas kernels, local(): pl.pallas_call(lambda *refs: kernel(n_span, *refs), out_shape=(out, out),...  48.7 us
    unnamed x21, local copies, waits for them, and re-layouts  9.79 us

profile of v1, /device:TPU:0, one launch (start us, length us, event | category | flops | bytes accessed | tf_op | source)
XLA Modules:
  0.0 59.1 jit_solution(8766595394184392194)
XLA Ops:
  0.6 0.8 %copy.13.refs_0_ = s32[12,3]{1,0:T(8,128)S(1)} copy(s32[12,3]{0,1:T(4,128)} %param.14) | data formatting | bytes 288 | tf_op args[3]
  1.4 0.0 copy-start
  1.4 1.0 %copy-done = bf16[4,128,384]{2,1,0:T(8,128)(2,1)S(1)} copy-done((bf16[4,128,384]{2,1,0:T(8,128)(2,1)S(1)}, bf16[4,128,384]{2,1,0:T(8,128)(2,1)}, u32[]{:S(2)}) %copy-start) | copy-done | bytes 393240
  2.4 0.0 copy-start.1
  2.4 0.9 %copy-done.1 = f32[4,4,3072]{2,1,0:T(4,128)S(1)} copy-done((f32[4,4,3072]{2,1,0:T(4,128)S(1)}, f32[4,4,3072]{2,1,0:T(4,128)}, u32[]{:S(2)}) %copy-start.1) | copy-done | bytes 196632
  3.3 0.0 copy-start.2
  3.3 0.9 %copy-done.2 = f32[4,4,3072]{2,1,0:T(4,128)S(1)} copy-done((f32[4,4,3072]{2,1,0:T(4,128)S(1)}, f32[4,4,3072]{2,1,0:T(4,128)}, u32[]{:S(2)}) %copy-start.2) | copy-done | bytes 196632
  4.3 0.0 copy-start.3
  4.3 0.9 %copy-done.3 = f32[3,12288]{1,0:T(4,128)S(1)} copy-done((f32[3,12288]{1,0:T(4,128)S(1)}, f32[3,12288]{1,0:T(4,128)}, u32[]{:S(2)}) %copy-start.3) | copy-done | bytes 147480
  5.2 0.0 copy-start.4
  5.2 0.9 %copy-done.4 = f32[3,4,3072]{2,1,0:T(4,128)S(1)} copy-done((f32[3,4,3072]{2,1,0:T(4,128)S(1)}, f32[3,4,3072]{2,1,0:T(4,128)}, u32[]{:S(2)}) %copy-start.4) | copy-done | bytes 147480
  6.1 0.0 copy-start.5
  6.1 0.9 %copy-done.5 = f32[2,128,128]{2,1,0:T(8,128)S(1)} copy-done((f32[2,128,128]{2,1,0:T(8,128)S(1)}, f32[2,128,128]{2,1,0:T(8,128)}, u32[]{:S(2)}) %copy-start.5) | copy-done | bytes 131096
  7.0 0.0 copy-start.6
  7.0 0.7 %copy-done.6 = f32[3072]{0:T(1024)S(1)} copy-done((f32[3072]{0:T(1024)S(1)}, f32[3072]{0:T(1024)}, u32[]{:S(2)}) %copy-start.6) | copy-done | bytes 12312
  7.7 0.0 copy-start.7
  7.7 0.7 %copy-done.7 = s32[768]{0:T(1024)S(1)} copy-done((s32[768]{0:T(1024)S(1)}, s32[768]{0:T(1024)}, u32[]{:S(2)}) %copy-start.7) | copy-done | bytes 3096
  8.4 0.0 copy-start.8
  8.4 0.7 %copy-done.8 = f32[3,3]{1,0:T(4,128)S(1)} copy-done((f32[3,3]{1,0:T(4,128)S(1)}, f32[3,3]{1,0:T(4,128)}, u32[]{:S(2)}) %copy-start.8) | copy-done | bytes 60
  9.1 48.7 %shard_map.122 = (f32[4,4,3072]{2,1,0:T(4,128)S(1)}, f32[4,4,3072]{2,1,0:T(4,128)S(1)}) custom-call(s32[12,3]{1,0:T(8,128)S(1)} %copy.13.refs_0_, f32[3,3]{1,0:T(4,128)S(1)} %copy-done.8, f32[4,4,3072]{2,1,0:T(4,128)S(1)} %copy-done.1, f32[4,4,3072]{2,1,0:T(4,128)S(1)} %copy-done.2, bf16[4,12,3,256,256]{4,3,2,1,0:T(8,128)(2,1)} %refs_4_.1, ...), custom_call_target="tpu_custom_call" | custom-call | tf_op jit(solution)/shard_map/pallas_call | solution.py:544
  57.8 0.7 %copy.16 = f32[4,4,3072]{2,1,0:T(4,128)} copy(f32[4,4,3072]{2,1,0:T(4,128)S(1)} %get-tuple-element.4) | data formatting | bytes 393216
  58.5 0.7 %copy.17 = f32[4,4,3072]{2,1,0:T(4,128)} copy(f32[4,4,3072]{2,1,0:T(4,128)S(1)} %get-tuple-element.5) | data formatting | bytes 393216
Async XLA Ops:
  1.4 1.0 %copy-start = (bf16[4,128,384]{2,1,0:T(8,128)(2,1)S(1)}, bf16[4,128,384]{2,1,0:T(8,128)(2,1)}, u32[]{:S(2)}) copy-start(bf16[4,128,384]{2,1,0:T(8,128)(2,1)} %constant.4.clone.refs_9_) | copy-start | bytes 1179652
  2.4 0.9 %copy-start.1 = (f32[4,4,3072]{2,1,0:T(4,128)S(1)}, f32[4,4,3072]{2,1,0:T(4,128)}, u32[]{:S(2)}) copy-start(f32[4,4,3072]{2,1,0:T(4,128)} %refs_2_.1) | copy-start | bytes 589828
  3.3 0.9 %copy-start.2 = (f32[4,4,3072]{2,1,0:T(4,128)S(1)}, f32[4,4,3072]{2,1,0:T(4,128)}, u32[]{:S(2)}) copy-start(f32[4,4,3072]{2,1,0:T(4,128)} %refs_3_.1) | copy-start | bytes 589828
  4.3 0.9 %copy-start.3 = (f32[3,12288]{1,0:T(4,128)S(1)}, f32[3,12288]{1,0:T(4,128)}, u32[]{:S(2)}) copy-start(f32[3,12288]{1,0:T(4,128)} %refs_8_.1) | copy-start | bytes 442372
  5.2 0.9 %copy-start.4 = (f32[3,4,3072]{2,1,0:T(4,128)S(1)}, f32[3,4,3072]{2,1,0:T(4,128)}, u32[]{:S(2)}) copy-start(f32[3,4,3072]{2,1,0:T(4,128)} %refs_6_.1) | copy-start | bytes 442372
  6.1 0.9 %copy-start.5 = (f32[2,128,128]{2,1,0:T(8,128)S(1)}, f32[2,128,128]{2,1,0:T(8,128)}, u32[]{:S(2)}) copy-start(f32[2,128,128]{2,1,0:T(8,128)} %constant.5.clone.refs_10_) | copy-start | bytes 393220
  7.0 0.7 %copy-start.6 = (f32[3072]{0:T(1024)S(1)}, f32[3072]{0:T(1024)}, u32[]{:S(2)}) copy-start(f32[3072]{0:T(1024)} %param.15) | copy-start | bytes 36868
  7.7 0.7 %copy-start.7 = (s32[768]{0:T(1024)S(1)}, s32[768]{0:T(1024)}, u32[]{:S(2)}) copy-start(s32[768]{0:T(1024)} %param.17) | copy-start | bytes 9220
  8.4 0.7 %copy-start.8 = (f32[3,3]{1,0:T(4,128)S(1)}, f32[3,3]{1,0:T(4,128)}, u32[]{:S(2)}) copy-start(f32[3,3]{1,0:T(4,128)} %refs_1_.1) | copy-start | bytes 112

commit v2 on v1

v2 whole, which is shorter than its diff:
```python
import math

import jax
import jax.numpy as jnp
import ml_dtypes
import numpy as np
from jax import lax
from jax.experimental import pallas as pl
from jax.experimental.pallas import tpu as pltpu
from jax.sharding import PartitionSpec as P

MESH = pl.DeviceIdType.MESH
F32 = jnp.float32
BF16 = jnp.bfloat16

INST = 32
PEERS = 8
OWN = 4
NOBJ = 4
ROWS = 3072
NB = 12
K = 3
TILE = 256
S_DEV = 768
RATE = 0.25
RELAX = 0.8


def split_const(a):
    hi = a.astype(ml_dtypes.bfloat16)
    lo = (a - hi.astype(np.float64)).astype(ml_dtypes.bfloat16)
    return np.concatenate([hi, hi, lo], axis=-1)


def constants():
    theta = 2.0 * math.pi * np.arange(INST) / INST
    half = INST // 2
    trans = np.concatenate(
        [
            np.cos(np.arange(half + 1)[:, None] * theta[None, :]),
            np.sin(np.arange(1, half)[:, None] * theta[None, :]),
        ]
    )
    spread = theta[:, None] - theta[None, :]
    orders = np.arange(1, half)[:, None, None]
    deriv = -(2.0 / INST) * np.sum(orders * np.sin(orders * spread[None]), axis=0)
    eye = np.eye(NOBJ)
    forward = np.kron(trans, eye)
    back = np.kron(trans.T, eye)
    forward_deriv = RATE * np.kron(trans @ deriv, eye)
    own_deriv = RATE * np.kron(deriv, eye)
    mats = [forward, back, forward_deriv, own_deriv]
    for c in range(3):
        spread_c = np.zeros((128, PEERS, 4, OWN))
        spread_c[:, :, c, :] = np.repeat(trans, NOBJ, axis=0).reshape(128, PEERS, OWN)
        mats.append(spread_c.reshape(128, 128))
    mats = np.stack([split_const(m) for m in mats])
    angle = np.repeat(theta, NOBJ)
    harm = np.stack([np.cos(angle), np.sin(angle)]).astype(np.float32)
    harm = np.ascontiguousarray(np.broadcast_to(harm[:, :, None], (2, 128, 128)))
    return mats, harm


def exact_dot(mat, x):
    hi = x.astype(BF16)
    lo = (x - hi.astype(F32)).astype(BF16)
    return jnp.dot(mat, jnp.concatenate([hi, lo, hi], axis=0), preferred_element_type=F32)


def kernel(
    n_span,
    cols_ref,
    tinv_ref,
    state_hbm,
    source_hbm,
    jac_hbm,
    pt_hbm,
    ct_hbm,
    rows_hbm,
    sw_hbm,
    mats_hbm,
    harm_hbm,
    adj_hbm,
    res_hbm,
    jbuf,
    st_v,
    src_v,
    ct_v,
    pt_v,
    rows_v,
    sw_v,
    mats_v,
    harm_v,
    out_a,
    out_r,
    s0,
    n0,
    n1,
    nf,
    w_v,
    base1,
    base2,
    xs,
    xb1,
    xb2,
    scal,
    yd,
    ctf,
    st1,
    ns,
    ds_,
    dr,
    as_,
    ar,
    r1s,
    r1r,
    r2s,
    r2r,
    j_sem,
    l_sem,
    st_send,
    st_recv,
    h0_send,
    h0_recv,
    b_send,
    b_recv,
    n_send,
    n_recv,
    h1_send,
    h1_recv,
    d_send,
    d_recv,
    a_send,
    a_recv,
    r1_send,
    r1_recv,
    r2_send,
    r2_recv,
):
    me = lax.axis_index("inst")
    sp = lax.axis_index("span")
    last = n_span - 1

    zero2 = jnp.zeros((2, 16, 128), BF16)
    n1[0, 6:8] = zero2
    n1[4, 0:2] = zero2
    for column in (0, NB + 1):
        n0[column] = jnp.zeros((16, TILE), BF16)

    barrier = pltpu.get_barrier_semaphore()

    def signal(i, s):
        pl.semaphore_signal(barrier, inc=1, device_id=(i, s), device_id_type=MESH)

    def peers(fn):
        @pl.loop(1, PEERS)
        def _(d):
            fn(jnp.bitwise_xor(me, d))

    def far_first(fn):
        for d in (5, 4, 7, 6, 3, 2, 1):
            fn(jnp.bitwise_xor(me, d))

    def spans(fn):
        @pl.loop(1, n_span)
        def _(d):
            fn(lax.rem(sp + d, n_span))

    peers(lambda p: signal(p, sp))
    spans(lambda q: signal(me, q))

    has_low = sp > 0
    has_high = sp < last
    def at_low(fn):
        @pl.when(has_low)
        def _():
            @pl.when(me < 2)
            def _():
                pl.loop(0, PEERS)(fn)

    def at_high(fn):
        @pl.when(has_high)
        def _():
            @pl.when(me >= PEERS - 2)
            def _():
                pl.loop(0, PEERS)(fn)

    def around(p):
        signal(p, lax.rem(sp + 1, n_span))
        signal(p, lax.rem(sp + n_span - 1, n_span))

    peers(around)

    local_in = [
        (state_hbm, st_v),
        (rows_hbm, rows_v),
        (sw_hbm.at[:, pl.ds(pl.multiple_of(sp * S_DEV, S_DEV), S_DEV)], sw_v),
        (harm_hbm, harm_v),
        (ct_hbm, ct_v),
        (source_hbm, src_v),
        (pt_hbm, pt_v),
        (mats_hbm, mats_v),
    ]
    loads = [pltpu.make_async_copy(a, b, l_sem.at[n]) for n, (a, b) in enumerate(local_in)]
    for c in loads:
        c.start()

    def jac_copy(b):
        return pltpu.make_async_copy(jac_hbm.at[:, b], jbuf.at[b], j_sem.at[b])

    @pl.loop(0, NB)
    def _(b):
        jac_copy(b).start()

    loads[0].wait()
    flat = jnp.concatenate([st_v[i] for i in range(OWN)], axis=0)
    for q in range(24):
        piece = flat[:, q * 128 : (q + 1) * 128]
        s0[q // 8, q % 8, 0:16] = piece
    loads[4].wait()
    flat_c = jnp.concatenate([ct_v[c] for c in range(3)] + [jnp.zeros((OWN, ROWS), F32)], axis=0)
    for q in range(24):
        s0[q // 8, q % 8, 16:32] = flat_c[:, q * 128 : (q + 1) * 128]
    for b in range(NB):
        n0[b + 1] = flat[:, b * TILE : (b + 1) * TILE].astype(BF16)

    def to(src, dst, send, recv, i, s):
        return pltpu.make_async_remote_copy(
            src_ref=src, dst_ref=dst, send_sem=send, recv_sem=recv, device_id=(i, s), device_id_type=MESH
        )

    def halo0_low():
        return to(n0.at[1], n0.at[NB + 1], h0_send.at[0], h0_recv.at[0], me, sp - 1)

    def halo0_high():
        return to(n0.at[NB], n0.at[0], h0_send.at[1], h0_recv.at[1], me, sp + 1)

    def state_out(p):
        return to(s0.at[:, p], xs.at[me], st_send.at[0], st_recv.at[0], p, sp)

    def base_out(k, t, p):
        src, dst = (base1, xb1) if k == 0 else (base2, xb2)
        return to(src.at[t, p], dst.at[me, t], b_send.at[k], b_recv.at[k], p, sp)

    def narrow_out(p):
        return to(ns.at[p], n1.at[pl.ds(1, 3), me], n_send.at[0], n_recv.at[0], p, sp)

    def halo1_low(p):
        return to(ns.at[p, 0], n1.at[4, me], h1_send.at[0], h1_recv.at[0], p, sp - 1)

    def halo1_high(p):
        return to(ns.at[p, 2], n1.at[0, me], h1_send.at[1], h1_recv.at[1], p, sp + 1)

    def deriv_out(p):
        return to(ds_.at[p], dr.at[:, me], d_send.at[0], d_recv.at[0], p, sp)

    def adj_out(p):
        return to(as_.at[p], ar.at[:, me], a_send.at[0], a_recv.at[0], p, sp)

    def sum1_out(k, q):
        return to(r1s.at[k], r1r.at[k, sp], r1_send.at[k], r1_recv.at[k], me, q)

    def sum2_out(k, p):
        return to(r2s.at[k], r2r.at[k, me], r2_send.at[k], r2_recv.at[k], p, sp)

    def arrived(dst, sem):
        pltpu.make_async_copy(dst, dst, sem).wait()

    loads[1].wait()
    loads[2].wait()
    rows = jnp.concatenate([rows_v[q : q + 1, :] for q in range(6)], axis=1)
    high, low = lax.div(rows, 128), lax.rem(rows, 128)
    tiles24 = lax.broadcasted_iota(jnp.int32, (24, S_DEV), 0)
    hit = jnp.broadcast_to(high, (24, S_DEV)) == tiles24
    spread = jnp.concatenate(
        [jnp.where(hit, jnp.broadcast_to(sw_v[c : c + 1, :], (24, S_DEV)), 0.0) for c in range(3)], axis=0
    )
    spread_hi = spread.astype(BF16)
    spread_lo = (spread - spread_hi.astype(F32)).astype(BF16)
    lane_hit = jnp.broadcast_to(low, (128, S_DEV)) == lax.broadcasted_iota(jnp.int32, (128, S_DEV), 0)
    lane_hit = jnp.where(lane_hit, 1.0, 0.0).astype(BF16)
    nt = (((1,), (1,)), ((), ()))
    w_v[...] = lax.dot_general(spread_hi, lane_hit, nt, preferred_element_type=F32) + lax.dot_general(
        spread_lo, lane_hit, nt, preferred_element_type=F32
    )

    lane8 = lax.broadcasted_iota(jnp.int32, (8, 128), 1)
    row8 = lax.rem(lax.broadcasted_iota(jnp.int32, (8, 128), 0), NOBJ)

    def load_row(accs):
        total = jnp.zeros((8, 128), F32)
        for c in range(3):
            col = jnp.sum(accs[c], axis=1, keepdims=True)
            total = total + jnp.where(lane8 == c * NOBJ + row8, jnp.broadcast_to(col, (8, 128)), 0.0)
        return jnp.sum(total, axis=0, keepdims=True)

    loads[3].wait()
    accs = []
    for c in range(3):
        acc = jnp.zeros((16, 128), F32)
        for q in range(24):
            acc = acc + s0[q // 8, q % 8, 0:16] * jnp.broadcast_to(w_v[c * 24 + q : c * 24 + q + 1, :], (16, 128))
        if c > 0:
            acc = acc * harm_v[c - 1, pl.ds(pl.multiple_of(me * 16, 16), 16), :]
        accs.append(acc[0:8] + acc[8:16])

    first_row = load_row(accs)
    pl.semaphore_wait(barrier, 3 * (PEERS - 1) + n_span - 1)

    @pl.when(has_low)
    def _():
        halo0_low().start()

    @pl.when(has_high)
    def _():
        halo0_high().start()

    def start_sum(k, row):
        r1s[k] = row
        r1r[k, pl.ds(sp, 1)] = row.reshape(1, 1, 128)
        spans(lambda q: sum1_out(k, q).start())

    start_sum(0, first_row)
    far_first(lambda p: state_out(p).start())
    xs[pl.ds(me, 1)] = s0[:, pl.ds(me, 1)].reshape(1, 3, 32, 128)

    def middle_sum(k):
        arrived(r1r.at[k, pl.ds(0, n_span - 1)], r1_recv.at[k])
        row = jnp.sum(r1r[k], axis=0)
        r2s[k] = row
        r2r[k, pl.ds(me, 1)] = row.reshape(1, 1, 128)
        far_first(lambda p: sum2_out(k, p).start())

    def multiplier(k):
        arrived(r2r.at[k, pl.ds(0, PEERS - 1)], r2_recv.at[k])
        row = jnp.broadcast_to(jnp.sum(r2r[k], axis=0), (8, 128))
        out = []
        for c in range(3):
            mask = jnp.zeros((8, 128), F32)
            for d in range(3):
                mask = jnp.where(lane8 == d * NOBJ + row8, tinv_ref[c, d], mask)
            col = jnp.sum(row * mask, axis=1, keepdims=True)
            out.append(jnp.broadcast_to(col, (8, 128)))
        return out

    inst_row = lax.div(lax.broadcasted_iota(jnp.int32, (16, TILE), 0), NOBJ)
    masks = [jnp.where(inst_row == i, 1.0, 0.0).astype(BF16) for i in range(OWN)]

    def product(b, narrow, base):
        blocks = [narrow[cols_ref[k, b] + 1] for k in range(K)]
        left = jnp.concatenate([blocks[k] * masks[i] for i in range(OWN) for k in range(K)], axis=1)
        acc = jnp.dot(left, jbuf[b].reshape(OWN * K * TILE, TILE), preferred_element_type=F32)
        rows = jnp.concatenate([src_v[i, :, b * TILE : (b + 1) * TILE] for i in range(OWN)], axis=0)
        value = rows - acc
        for half in range(2):
            q = 2 * b + half
            base[q // 8, q % 8] = value[:, half * 128 : (half + 1) * 128]

    def sweep_products(k, narrow, base, landed):
        for t in range(3):
            for b in range(4 * t, 4 * t + 4):
                if k == 0:
                    jac_copy(b).wait()
                product(b, narrow, base)
            far_first(lambda p: base_out(k, t, p).start())
            landed[pl.ds(me, 1), t] = base[t, pl.ds(me, 1)]
            if t == k:
                middle_sum(k)

    def wide(ref):
        return jnp.concatenate([ref[:, t].reshape(128, 128) for t in range(3)], axis=1)

    def wide_part(ref, first):
        parts = [ref[:, t, first : first + 16].reshape(128, 128) for t in range(3)]
        return jnp.concatenate(parts, axis=1)

    def add_control(k):
        mult = multiplier(k)
        total = yd[...].reshape(16, 8, 384)
        for c in range(3):
            total = total - ctf[c].reshape(16, 8, 384) * jnp.concatenate([mult[c]] * 3, axis=1)[None]
        yd[...] = total.reshape(128, 384)
        return mult

    @pl.when(has_high)
    def _():
        arrived(n0.at[NB + 1], h0_recv.at[0])

    @pl.when(has_low)
    def _():
        arrived(n0.at[0], h0_recv.at[1])

    loads[5].wait()
    sweep_products(0, n0, base1, xb1)

    for c in loads[6:]:
        c.wait()
    order = lax.div(lax.broadcasted_iota(jnp.int32, (128, 128), 0), NOBJ)
    freq = jnp.where(order > INST // 2, order - INST // 2, order)
    ends = jnp.logical_or(freq == 0, freq == INST // 2)
    weight = jnp.where(ends, RELAX / INST, 2.0 * RELAX / INST)
    offset = RATE * freq.astype(F32)
    for t in range(3):
        pt = jnp.broadcast_to(pt_v[t, pl.ds(me, 1), :], (128, 128))
        scal[:, t * 128 : (t + 1) * 128] = weight / (pt + offset)
    arrived(xs.at[pl.ds(0, PEERS - 1)], st_recv.at[0])
    state0 = wide_part(xs, 0)
    yd[...] = exact_dot(mats_v[2], state0)
    control = wide_part(xs, 16)
    for c in range(3):
        ctf[c] = exact_dot(mats_v[4 + c], control)
    add_control(0)

    def wait_base(k):
        arrived((xb1 if k == 0 else xb2).at[pl.ds(0, PEERS - 1)], b_recv.at[k])

    wait_base(0)
    spectrum = exact_dot(mats_v[0], wide(xb1)) + yd[...]
    state1 = wide_part(xs, 0) + exact_dot(mats_v[1], spectrum * scal[...])
    st1[...] = state1
    for t in range(3):
        piece = state1[:, t * 128 : (t + 1) * 128]
        ns[:, t] = piece.astype(BF16).reshape(PEERS, 16, 128)
    far_first(lambda p: narrow_out(p).start())

    at_low(lambda p: halo1_low(p).start())
    at_high(lambda p: halo1_high(p).start())

    n1[pl.ds(1, 3), pl.ds(me, 1)] = ns[pl.ds(me, 1)].reshape(3, 1, 16, 128)

    accs = []
    for c in range(3):
        acc = jnp.zeros((128, 128), F32)
        for t in range(3):
            weight = w_v[pl.ds(c * 24 + t * 8 + me, 1), :]
            acc = acc + state1[:, t * 128 : (t + 1) * 128] * jnp.broadcast_to(weight, (128, 128))
        if c > 0:
            acc = acc * harm_v[c - 1]
        accs.append(jnp.sum(acc.reshape(16, 8, 128), axis=0))
    start_sum(1, load_row(accs))

    yd[...] = exact_dot(mats_v[2], state1)
    derived = exact_dot(mats_v[3], state1)
    for t in range(3):
        ds_[:, t] = derived[:, t * 128 : (t + 1) * 128].reshape(PEERS, 16, 128)
    far_first(lambda p: deriv_out(p).start())
    dr[:, pl.ds(me, 1)] = ds_[pl.ds(me, 1)].reshape(3, 1, 16, 128)

    arrived(n1.at[pl.ds(1, 3), pl.ds(0, PEERS - 1)], n_recv.at[0])

    @pl.when(has_high)
    def _():
        arrived(n1.at[4, pl.ds(0, 2)], h1_recv.at[0])

    @pl.when(has_low)
    def _():
        arrived(n1.at[0, pl.ds(PEERS - 2, 2)], h1_recv.at[1])

    for column in range(NB + 2):
        slot = 2 * column + 6
        left, right = n1[slot // 8, slot % 8], n1[slot // 8, slot % 8 + 1]
        nf[column] = jnp.concatenate([left, right], axis=1)

    sweep_products(1, nf, base2, xb2)
    mult = add_control(1)

    wait_base(1)
    spectrum = exact_dot(mats_v[0], wide(xb2)) + yd[...]
    final = st1[...] + exact_dot(mats_v[1], spectrum * scal[...])
    for t in range(3):
        as_[:, t] = final[:, t * 128 : (t + 1) * 128].reshape(PEERS, 16, 128)
    far_first(lambda p: adj_out(p).start())
    ar[:, pl.ds(me, 1)] = as_[pl.ds(me, 1)].reshape(3, 1, 16, 128)

    def drain():
        @pl.when(has_low)
        def _():
            halo0_low().wait_send()

        @pl.when(has_high)
        def _():
            halo0_high().wait_send()

        @pl.when(has_low)
        def _():
            @pl.when(me < 2)
            def _():
                arrived(ns.at[:, 0], h1_send.at[0])

        @pl.when(has_high)
        def _():
            @pl.when(me >= PEERS - 2)
            def _():
                arrived(ns.at[:, 2], h1_send.at[1])

        arrived(s0.at[:, pl.ds(0, PEERS - 1)], st_send.at[0])
        arrived(ns.at[pl.ds(0, PEERS - 1)], n_send.at[0])
        arrived(ds_.at[pl.ds(0, PEERS - 1)], d_send.at[0])
        for k, base in ((0, base1), (1, base2)):
            arrived(base.at[:, pl.ds(0, PEERS - 1)], b_send.at[k])
            arrived(r1r.at[k, pl.ds(0, n_span - 1)], r1_send.at[k])
            arrived(r2r.at[k, pl.ds(0, PEERS - 1)], r2_send.at[k])

    def put(out, fn):
        for q in range(24):
            value = fn(q // 8, q % 8)
            for i in range(OWN):
                out[i, :, q * 128 : (q + 1) * 128] = value[i * NOBJ : (i + 1) * NOBJ, :]

    mult16 = [jnp.concatenate([m, m], axis=0) for m in mult]
    first_half = lax.div(lax.broadcasted_iota(jnp.int32, (8, 128), 0), NOBJ) == 0

    def residual_tile(t, p):
        q = t * 8 + p
        lanes = slice(q * 128, (q + 1) * 128)
        value = base2[t, p] + dr[t, p]
        for c in range(3):
            parts = []
            for h in range(2):
                first = jnp.broadcast_to(ct_v[c, 2 * h : 2 * h + 1, lanes], (8, 128))
                second = jnp.broadcast_to(ct_v[c, 2 * h + 1 : 2 * h + 2, lanes], (8, 128))
                parts.append(jnp.where(first_half, first, second))
            value = value - jnp.concatenate(parts, axis=0) * mult16[c]
        return value

    arrived(dr.at[:, pl.ds(0, PEERS - 1)], d_recv.at[0])
    put(out_r, residual_tile)
    write_r = pltpu.make_async_copy(out_r, res_hbm, l_sem.at[0])
    write_r.start()
    drain()
    arrived(ar.at[:, pl.ds(0, PEERS - 1)], a_recv.at[0])
    put(out_a, lambda t, p: ar[t, p])
    write_a = pltpu.make_async_copy(out_a, adj_hbm, l_sem.at[1])
    write_a.start()

    arrived(as_.at[pl.ds(0, PEERS - 1)], a_send.at[0])
    write_r.wait()
    write_a.wait()


def solution(mesh):
    n_span = mesh.shape["span"]
    mats, harm = constants()

    def local(
        adjoint_start,
        source,
        jacobian_tiles,
        tile_columns,
        pseudo_time,
        control_terms,
        surface_rows,
        surface_weight,
        trim_inverse,
    ):
        any_spec = pl.BlockSpec(memory_space=pl.ANY)
        smem = pl.BlockSpec(memory_space=pltpu.SMEM)
        dma = pltpu.SemaphoreType.DMA
        vm = pltpu.VMEM
        out = jax.ShapeDtypeStruct((OWN, NOBJ, ROWS), F32)
        return pl.pallas_call(
            lambda *refs: kernel(n_span, *refs),
            out_shape=(out, out),
            in_specs=[smem, smem] + [any_spec] * 9,
            out_specs=(any_spec, any_spec),
            scratch_shapes=[
                vm((NB, OWN, K, TILE, TILE), BF16),
                vm((OWN, NOBJ, ROWS), F32),
                vm((OWN, NOBJ, ROWS), F32),
                vm((3, OWN, ROWS), F32),
                vm((3, 8, 128), F32),
                vm((6, 128), jnp.int32),
                vm((3, S_DEV), F32),
                vm((7, 128, 384), BF16),
                vm((2, 128, 128), F32),
                vm((OWN, NOBJ, ROWS), F32),
                vm((OWN, NOBJ, ROWS), F32),
                vm((3, 8, 32, 128), F32),
                vm((NB + 2, 16, TILE), BF16),
                vm((5, 8, 16, 128), BF16),
                vm((NB + 2, 16, TILE), BF16),
                vm((72, 128), F32),
                vm((3, 8, 16, 128), F32),
                vm((3, 8, 16, 128), F32),
                vm((8, 3, 32, 128), F32),
                vm((8, 3, 16, 128), F32),
                vm((8, 3, 16, 128), F32),
                vm((128, 384), F32),
                vm((128, 384), F32),
                vm((3, 128, 384), F32),
                vm((128, 384), F32),
                vm((8, 3, 16, 128), BF16),
                vm((8, 3, 16, 128), F32),
                vm((3, 8, 16, 128), F32),
                vm((8, 3, 16, 128), F32),
                vm((3, 8, 16, 128), F32),
                vm((2, 1, 128), F32),
                vm((2, n_span, 1, 128), F32),
                vm((2, 1, 128), F32),
                vm((2, PEERS, 1, 128), F32),
                dma((NB,)),
                dma((8,)),
                dma((1,)),
                dma((1,)),
                dma((2,)),
                dma((2,)),
                dma((2,)),
                dma((2,)),
                dma((1,)),
                dma((1,)),
                dma((2,)),
                dma((2,)),
                dma((1,)),
                dma((1,)),
                dma((1,)),
                dma((1,)),
                dma((2,)),
                dma((2,)),
                dma((2,)),
                dma((2,)),
            ],
            compiler_params=pltpu.CompilerParams(
                collective_id=0, has_side_effects=True, vmem_limit_bytes=62 * 1024 * 1024
            ),
        )(
            tile_columns.T,
            trim_inverse,
            adjoint_start,
            source,
            jacobian_tiles,
            pseudo_time.reshape(3, 8, 128),
            control_terms,
            surface_rows.reshape(6, 128),
            surface_weight,
            jnp.asarray(mats),
            jnp.asarray(harm),
        )

    return jax.shard_map(
        local,
        mesh=mesh,
        in_specs=(
            P("inst", None, "span"),
            P("inst", None, "span"),
            P("inst", "span", None, None, None),
            P("span", None),
            P("span"),
            P(None, "inst", "span"),
            P("span"),
            P(),
            P(),
        ),
        out_specs=(P("inst", None, "span"), P("inst", None, "span")),
        check_vma=False,
    )
```

time: 59.5 us -> 45.2 us (0.76)
  the two profiles are of different devices: /device:TPU:0 before, /device:TPU:1 now
where the time goes in v2:
time: 45.2 us; the launch traced here: 45 us
  Pallas kernels  41.1 us (91%)
  local copies, waits for them, and re-layouts  3.23 us (7%)
  between operations  0.64 us (1%)
    pallas_call x1, Pallas kernels, local(): pl.pallas_call(lambda *refs: kernel(n_span, *refs), out_shape=(out, out),...  41.1 us
    unnamed x2, local copies, waits for them, and re-layouts  3.23 us

profile of v2, /device:TPU:1, one launch (start us, length us, event | category | flops | bytes accessed | tf_op | source)
XLA Modules:
  0.0 45.0 jit_solution(11130834837074946996)
XLA Ops:
  0.6 41.1 %shard_map.122 = (f32[4,4,3072]{2,1,0:T(4,128)}, f32[4,4,3072]{2,1,0:T(4,128)}) custom-call(s32[3,12]{1,0:T(4,128)} %bitcast.5, f32[3,3]{1,0:T(4,128)} %refs_1_.1, f32[4,4,3072]{2,1,0:T(4,128)} %refs_2_.1, f32[4,4,3072]{2,1,0:T(4,128)} %refs_3_.1, bf16[4,12,3,256,256]{4,3,2,1,0:T(8,128)(2,1)} %refs_4_.1, f32[3,8,128]{2,1,0:T(8,128)} %bitcast.3, ...), custom_call_target="tpu_custom_call" | custom-call | tf_op jit(solution)/shard_map/pallas_call | solution.py:561
  41.7 1.6 %copy.15 = f32[4,4,3072]{2,1,0:T(4,128)} copy(f32[4,4,3072]{2,1,0:T(4,128)} %get-tuple-element.4) | data formatting | bytes 393216
  43.4 1.6 %copy.16 = f32[4,4,3072]{2,1,0:T(4,128)} copy(f32[4,4,3072]{2,1,0:T(4,128)} %get-tuple-element.5) | data formatting | bytes 393216

commit v3 on v2

--- a/solution.py
+++ b/solution.py
@@ -141,56 +141,6 @@
     sp = lax.axis_index("span")
     last = n_span - 1
 
-    zero2 = jnp.zeros((2, 16, 128), BF16)
-    n1[0, 6:8] = zero2
-    n1[4, 0:2] = zero2
-    for column in (0, NB + 1):
-        n0[column] = jnp.zeros((16, TILE), BF16)
-
-    barrier = pltpu.get_barrier_semaphore()
-
-    def signal(i, s):
-        pl.semaphore_signal(barrier, inc=1, device_id=(i, s), device_id_type=MESH)
-
-    def peers(fn):
-        @pl.loop(1, PEERS)
-        def _(d):
-            fn(jnp.bitwise_xor(me, d))
-
-    def far_first(fn):
-        for d in (5, 4, 7, 6, 3, 2, 1):
-            fn(jnp.bitwise_xor(me, d))
-
-    def spans(fn):
-        @pl.loop(1, n_span)
-        def _(d):
-            fn(lax.rem(sp + d, n_span))
-
-    peers(lambda p: signal(p, sp))
-    spans(lambda q: signal(me, q))
-
-    has_low = sp > 0
-    has_high = sp < last
-    def at_low(fn):
-        @pl.when(has_low)
-        def _():
-            @pl.when(me < 2)
-            def _():
-                pl.loop(0, PEERS)(fn)
-
-    def at_high(fn):
-        @pl.when(has_high)
-        def _():
-            @pl.when(me >= PEERS - 2)
-            def _():
-                pl.loop(0, PEERS)(fn)
-
-    def around(p):
-        signal(p, lax.rem(sp + 1, n_span))
-        signal(p, lax.rem(sp + n_span - 1, n_span))
-
-    peers(around)
-
     local_in = [
         (state_hbm, st_v),
         (rows_hbm, rows_v),
@@ -212,6 +162,56 @@
     def _(b):
         jac_copy(b).start()
 
+    zero2 = jnp.zeros((2, 16, 128), BF16)
+    n1[0, 6:8] = zero2
+    n1[4, 0:2] = zero2
+    for column in (0, NB + 1):
+        n0[column] = jnp.zeros((16, TILE), BF16)
+
+    barrier = pltpu.get_barrier_semaphore()
+
+    def signal(i, s):
+        pl.semaphore_signal(barrier, inc=1, device_id=(i, s), device_id_type=MESH)
+
+    def peers(fn):
+        @pl.loop(1, PEERS)
+        def _(d):
+            fn(jnp.bitwise_xor(me, d))
+
+    def far_first(fn):
+        for d in (5, 4, 7, 6, 3, 2, 1):
+            fn(jnp.bitwise_xor(me, d))
+
+    def spans(fn):
+        @pl.loop(1, n_span)
+        def _(d):
+            fn(lax.rem(sp + d, n_span))
+
+    peers(lambda p: signal(p, sp))
+    spans(lambda q: signal(me, q))
+
+    has_low = sp > 0
+    has_high = sp < last
+    def at_low(fn):
+        @pl.when(has_low)
+        def _():
+            @pl.when(me < 2)
+            def _():
+                pl.loop(0, PEERS)(fn)
+
+    def at_high(fn):
+        @pl.when(has_high)
+        def _():
+            @pl.when(me >= PEERS - 2)
+            def _():
+                pl.loop(0, PEERS)(fn)
+
+    def around(p):
+        signal(p, lax.rem(sp + 1, n_span))
+        signal(p, lax.rem(sp + n_span - 1, n_span))
+
+    peers(around)
+
     loads[0].wait()
     flat = jnp.concatenate([st_v[i] for i in range(OWN)], axis=0)
     for q in range(24):
@@ -224,6 +224,8 @@
     for b in range(NB):
         n0[b + 1] = flat[:, b * TILE : (b + 1) * TILE].astype(BF16)
 
+    pl.semaphore_wait(barrier, 3 * (PEERS - 1) + n_span - 1)
+
     def to(src, dst, send, recv, i, s):
         return pltpu.make_async_remote_copy(
             src_ref=src, dst_ref=dst, send_sem=send, recv_sem=recv, device_id=(i, s), device_id_type=MESH
@@ -265,6 +267,14 @@
 
     def arrived(dst, sem):
         pltpu.make_async_copy(dst, dst, sem).wait()
+
+    @pl.when(has_low)
+    def _():
+        halo0_low().start()
+
+    @pl.when(has_high)
+    def _():
+        halo0_high().start()
 
     loads[1].wait()
     loads[2].wait()
@@ -304,23 +314,12 @@
             acc = acc * harm_v[c - 1, pl.ds(pl.multiple_of(me * 16, 16), 16), :]
         accs.append(acc[0:8] + acc[8:16])
 
-    first_row = load_row(accs)
-    pl.semaphore_wait(barrier, 3 * (PEERS - 1) + n_span - 1)
-
-    @pl.when(has_low)
-    def _():
-        halo0_low().start()
-
-    @pl.when(has_high)
-    def _():
-        halo0_high().start()
-
     def start_sum(k, row):
         r1s[k] = row
         r1r[k, pl.ds(sp, 1)] = row.reshape(1, 1, 128)
         spans(lambda q: sum1_out(k, q).start())
 
-    start_sum(0, first_row)
+    start_sum(0, load_row(accs))
     far_first(lambda p: state_out(p).start())
     xs[pl.ds(me, 1)] = s0[:, pl.ds(me, 1)].reshape(1, 3, 32, 128)
 
@@ -364,7 +363,7 @@
                 product(b, narrow, base)
             far_first(lambda p: base_out(k, t, p).start())
             landed[pl.ds(me, 1), t] = base[t, pl.ds(me, 1)]
-            if t == k:
+            if t == 2 - k:
                 middle_sum(k)
 
     def wide(ref):
@@ -538,6 +537,11 @@
     write_a.wait()
 
 
+def hand_over(a_in, r_in, a_out, r_out):
+    a_out[...] = a_in[...]
+    r_out[...] = r_in[...]
+
+
 def solution(mesh):
     n_span = mesh.shape["span"]
     mats, harm = constants()
@@ -555,10 +559,11 @@
     ):
         any_spec = pl.BlockSpec(memory_space=pl.ANY)
         smem = pl.BlockSpec(memory_space=pltpu.SMEM)
+        vmem_spec = pl.BlockSpec(memory_space=pltpu.VMEM)
         dma = pltpu.SemaphoreType.DMA
         vm = pltpu.VMEM
         out = jax.ShapeDtypeStruct((OWN, NOBJ, ROWS), F32)
-        return pl.pallas_call(
+        both = pl.pallas_call(
             lambda *refs: kernel(n_span, *refs),
             out_shape=(out, out),
             in_specs=[smem, smem] + [any_spec] * 9,
@@ -635,6 +640,12 @@
             jnp.asarray(mats),
             jnp.asarray(harm),
         )
+        return pl.pallas_call(
+            hand_over,
+            out_shape=(out, out),
+            in_specs=[vmem_spec, vmem_spec],
+            out_specs=(vmem_spec, vmem_spec),
+        )(*both)
 
     return jax.shard_map(
         local,

time: 45.2 us -> 43.6 us (0.965)
  local copies, waits for them, and re-layouts: 3.23 us -> 0 us
  Pallas kernels: 41.1 us -> 42.8 us
    unnamed x2 -> x0, local copies, waits for them, and re-layouts: 3.23 us -> none
    pallas_call x0 -> x1, Pallas kernels: none -> 1.78 us  [local(): pl.pallas_call(hand_over, out_shape=(out, out), in_specs=[vmem_spec, vmem...]
where the time goes in v3:
time: 43.6 us; the launch traced here: 43.5 us
  Pallas kernels  42.8 us (98%)
  between operations  0.64 us (1%)
    pallas_call x1, Pallas kernels, local(): pl.pallas_call(lambda *refs: kernel(n_span, *refs), out_shape=(out, out),...  41.1 us
    pallas_call x1, Pallas kernels, local(): pl.pallas_call(hand_over, out_shape=(out, out), in_specs=[vmem_spec, vmem...  1.78 us

profile of v3, /device:TPU:1, one launch (start us, length us, event | category | flops | bytes accessed | tf_op | source)
XLA Modules:
  0.0 43.5 jit_solution(8318374930820155385)
XLA Ops:
  0.6 41.1 %shard_map.122 = (f32[4,4,3072]{2,1,0:T(4,128)}, f32[4,4,3072]{2,1,0:T(4,128)}) custom-call(s32[3,12]{1,0:T(4,128)} %bitcast.5, f32[3,3]{1,0:T(4,128)} %refs_1_.1, f32[4,4,3072]{2,1,0:T(4,128)} %refs_2_.1, f32[4,4,3072]{2,1,0:T(4,128)} %refs_3_.1, bf16[4,12,3,256,256]{4,3,2,1,0:T(8,128)(2,1)} %refs_4_.1, f32[3,8,128]{2,1,0:T(8,128)} %bitcast.3, ...), custom_call_target="tpu_custom_call" | custom-call | tf_op jit(solution)/shard_map/pallas_call | solution.py:566
  41.7 1.8 %shard_map.123 = (f32[4,4,3072]{2,1,0:T(4,128)}, f32[4,4,3072]{2,1,0:T(4,128)}) custom-call(f32[4,4,3072]{2,1,0:T(4,128)} %get-tuple-element.4.a_in, f32[4,4,3072]{2,1,0:T(4,128)} %get-tuple-element.5.r_in), custom_call_target="tpu_custom_call" | custom-call | tf_op jit(solution)/shard_map/pallas_call | solution.py:643

commit v4 on v3

--- a/solution.py
+++ b/solution.py
@@ -174,8 +174,7 @@
         pl.semaphore_signal(barrier, inc=1, device_id=(i, s), device_id_type=MESH)
 
     def peers(fn):
-        @pl.loop(1, PEERS)
-        def _(d):
+        for d in (5, 4, 7, 6, 3, 2, 1):
             fn(jnp.bitwise_xor(me, d))
 
     def far_first(fn):
@@ -183,8 +182,7 @@
             fn(jnp.bitwise_xor(me, d))
 
     def spans(fn):
-        @pl.loop(1, n_span)
-        def _(d):
+        for d in range(1, n_span):
             fn(lax.rem(sp + d, n_span))
 
     peers(lambda p: signal(p, sp))
@@ -439,28 +437,28 @@
     start_sum(1, load_row(accs))
 
     yd[...] = exact_dot(mats_v[2], state1)
-    derived = exact_dot(mats_v[3], state1)
+    arrived(n1.at[pl.ds(1, 3), pl.ds(0, PEERS - 1)], n_recv.at[0])
+
+    @pl.when(has_high)
+    def _():
+        arrived(n1.at[4, pl.ds(0, 2)], h1_recv.at[0])
+
+    @pl.when(has_low)
+    def _():
+        arrived(n1.at[0, pl.ds(PEERS - 2, 2)], h1_recv.at[1])
+
+    for column in range(NB + 2):
+        slot = 2 * column + 6
+        left, right = n1[slot // 8, slot % 8], n1[slot // 8, slot % 8 + 1]
+        nf[column] = jnp.concatenate([left, right], axis=1)
+
+    sweep_products(1, nf, base2, xb2)
+    derived = exact_dot(mats_v[3], st1[...])
     for t in range(3):
         ds_[:, t] = derived[:, t * 128 : (t + 1) * 128].reshape(PEERS, 16, 128)
     far_first(lambda p: deriv_out(p).start())
     dr[:, pl.ds(me, 1)] = ds_[pl.ds(me, 1)].reshape(3, 1, 16, 128)
 
-    arrived(n1.at[pl.ds(1, 3), pl.ds(0, PEERS - 1)], n_recv.at[0])
-
-    @pl.when(has_high)
-    def _():
-        arrived(n1.at[4, pl.ds(0, 2)], h1_recv.at[0])
-
-    @pl.when(has_low)
-    def _():
-        arrived(n1.at[0, pl.ds(PEERS - 2, 2)], h1_recv.at[1])
-
-    for column in range(NB + 2):
-        slot = 2 * column + 6
-        left, right = n1[slot // 8, slot % 8], n1[slot // 8, slot % 8 + 1]
-        nf[column] = jnp.concatenate([left, right], axis=1)
-
-    sweep_products(1, nf, base2, xb2)
     mult = add_control(1)
 
     wait_base(1)

time: 43.6 us -> 43.6 us (level)
  no operation moved by 1% of the time
where the time goes in v4:
time: 43.6 us; the launch traced here: 43.4 us
  Pallas kernels  42.8 us (98%)
  between operations  0.64 us (1%)
    pallas_call x1, Pallas kernels, local(): pl.pallas_call(lambda *refs: kernel(n_span, *refs), out_shape=(out, out),...  41 us
    pallas_call x1, Pallas kernels, local(): pl.pallas_call(hand_over, out_shape=(out, out), in_specs=[vmem_spec, vmem...  1.78 us

profile of v4, /device:TPU:1, one launch (start us, length us, event | category | flops | bytes accessed | tf_op | source)
XLA Modules:
  0.0 43.4 jit_solution(716482422305149644)
XLA Ops:
  0.6 41.0 %shard_map.122 = (f32[4,4,3072]{2,1,0:T(4,128)}, f32[4,4,3072]{2,1,0:T(4,128)}) custom-call(s32[3,12]{1,0:T(4,128)} %bitcast.5, f32[3,3]{1,0:T(4,128)} %refs_1_.1, f32[4,4,3072]{2,1,0:T(4,128)} %refs_2_.1, f32[4,4,3072]{2,1,0:T(4,128)} %refs_3_.1, bf16[4,12,3,256,256]{4,3,2,1,0:T(8,128)(2,1)} %refs_4_.1, f32[3,8,128]{2,1,0:T(8,128)} %bitcast.3, ...), custom_call_target="tpu_custom_call" | custom-call | tf_op jit(solution)/shard_map/pallas_call | solution.py:564
  41.6 1.8 %shard_map.123 = (f32[4,4,3072]{2,1,0:T(4,128)}, f32[4,4,3072]{2,1,0:T(4,128)}) custom-call(f32[4,4,3072]{2,1,0:T(4,128)} %get-tuple-element.4.a_in, f32[4,4,3072]{2,1,0:T(4,128)} %get-tuple-element.5.r_in), custom_call_target="tpu_custom_call" | custom-call | tf_op jit(solution)/shard_map/pallas_call | solution.py:641
